TPU v7x, 32 devices: a whole 2x2x4 slice. The times are simulated.
32 devices in a mesh: ev: 2 (over y), gx: 4 (over z), gy: 4 (over x, core).
Axes of the slice: x: 2, y: 2, z: 4, core: 2. Of those that a mesh axis runs over, the one named last changes fastest.
Arguments:
- forward_state: float32 [2, 9, 4, 64, 512], P('ev', None, None, 'gx', 'gy'), may hold values from -6 to 6
- adjoint_state: float32 [2, 9, 4, 64, 512], P('ev', None, None, 'gx', 'gy'), may hold values from -6 to 6
- first_lame_parameter: float32 [4, 64, 512], P(None, 'gx', 'gy'), may hold values from 0.5 to 2
- shear_stiffness: float32 [4, 64, 512], P(None, 'gx', 'gy'), may hold values from 0.5 to 1.5
- buoyancy: float32 [4, 64, 512], P(None, 'gx', 'gy'), may hold values from 0.5 to 1.5
- layer_mask: int32 [4, 64, 512], P(None, 'gx', 'gy'), may hold values 0 or 1
- layer_element: int32 [4, 64, 512], P(None, 'gx', 'gy'), may hold values from 0 to 511
- layer_forces: float32 [2, 3, 512], P('ev'), may hold values from -24 to 24
Outputs:
- forward_next: float32 [2, 9, 4, 64, 512], P('ev', None, None, 'gx', 'gy')
- kernels: float32 [3, 4, 64, 512], P(None, None, 'gx', 'gy')
All inputs are finite; a program needn't handle non-finite values. No bound on the sum of `layer_mask` on one device may be relied on, other than what follows from the above.
Results may differ from a plain program's by a relative error of at most 0.00002.
Values sent between devices are 32-bit elements; how exact they have to be, the bound alone decides.
A program may use at most 64 MiB of HBM per device.

v0:
```python
import functools

import jax
import jax.numpy as jnp
from jax import lax
from jax.experimental import pallas as pl
from jax.experimental.pallas import tpu as pltpu
from jax.sharding import PartitionSpec as P

MESH = pl.DeviceIdType.MESH
INNER = 9.0 / 8.0
OUTER = -1.0 / 24.0
STEP = 0.15
PAD = 8


def depth_ahead(f):
    zero = jnp.zeros_like(f[:, :1])
    p1 = jnp.concatenate([f[:, 1:], zero], 1)
    p2 = jnp.concatenate([f[:, 2:], zero, zero], 1)
    m1 = jnp.concatenate([zero, f[:, :-1]], 1)
    return INNER * (p1 - f) + OUTER * (p2 - m1)


def depth_behind(f):
    zero = jnp.zeros_like(f[:, :1])
    p1 = jnp.concatenate([f[:, 1:], zero], 1)
    m1 = jnp.concatenate([zero, f[:, :-1]], 1)
    m2 = jnp.concatenate([zero, zero, f[:, :-2]], 1)
    return INNER * (f - m1) + OUTER * (p1 - m2)


def turn(f, shift):
    return pltpu.roll(f, shift % f.shape[-1], f.ndim - 1)


def lane_ahead(f):
    return INNER * (turn(f, -1) - f) + OUTER * (turn(f, -2) - turn(f, 1))


def lane_behind(f):
    return INNER * (f - turn(f, 1)) + OUTER * (turn(f, -1) - turn(f, 2))


def row_ahead(ref, c, rows):
    def at(k):
        return ref[:, c, :, pl.ds(PAD + k, rows), :]

    return INNER * (at(1) - at(0)) + OUTER * (at(2) - at(-1))


def row_behind(ref, c, rows):
    def at(k):
        return ref[:, c, :, pl.ds(PAD + k, rows), :]

    return INNER * (at(0) - at(-1)) + OUTER * (at(1) - at(-2))


def pack_lanes(fields, lanes):
    slot_of = lanes // 4
    packed = jnp.zeros(lanes.shape, jnp.float32)
    k = 0
    for f in fields:
        for s in range(f.shape[0]):
            for z in range(f.shape[1]):
                packed = jnp.where(slot_of == k, turn(f[s, z], 4 * k + 2), packed)
                k += 1
    return packed


def lane_fix(own, left, right, lanes, per, ahead):
    place = lanes % 4
    kind = lanes // (4 * per)
    is_ahead = functools.reduce(
        jnp.logical_or, [kind == c for c, flag in enumerate(ahead) if flag]
    )

    def weight(ahead_at, behind_at):
        def table(entries):
            out = jnp.zeros(lanes.shape, jnp.float32)
            for j, value in entries:
                out = jnp.where(place == j, value, out)
            return out

        return jnp.where(is_ahead, table(ahead_at), table(behind_at))

    m = jnp.where(place < 2, left, right) - own
    return (
        weight([(0, OUTER), (1, OUTER)], []) * turn(m, -2)
        + weight([(1, INNER)], [(1, OUTER)]) * turn(m, -1)
        + weight([(2, -OUTER)], [(2, -INNER)]) * turn(m, 1)
        + weight([], [(2, -OUTER), (3, -OUTER)]) * turn(m, 2)
    )


def unpack_lanes(fix, first, count, depth, edge):
    parts = []
    for s in range(2):
        parts.append(
            jnp.stack(
                [
                    jnp.where(edge, turn(fix, -(4 * (first + s * depth + z) + 2)), 0.0)
                    for z in range(depth)
                ]
            )
        )
    return jnp.stack(parts)


def kernel(
    sizes,
    fwd,
    adj,
    lame_in,
    shear_in,
    buoy_in,
    mask_in,
    elem_in,
    table_in,
    new,
    mine,
    theirs,
    theirs_rows,
    theirs_lanes,
    ext,
    rest,
    lame,
    shear,
    buoy,
    mask,
    elem,
    table,
    vext,
    sums,
    pack,
    from_left,
    from_right,
    vint,
    early,
    mine_lanes,
    load_sem,
    row_send,
    row_recv,
    lane_send,
    lane_recv,
    ev_send,
    ev_recv,
):
    n_ev, n_gx, n_gy = sizes
    ev, gx, gy = lax.axis_index("ev"), lax.axis_index("gx"), lax.axis_index("gy")
    _, _, depth, rows, cols = rest.shape
    per = 2 * depth

    barrier = pltpu.get_barrier_semaphore()
    has = {
        "up": gx > 0,
        "down": gx < n_gx - 1,
        "left": gy > 0,
        "right": gy < n_gy - 1,
    }
    where = {
        "up": {"gx": gx - 1},
        "down": {"gx": gx + 1},
        "left": {"gy": gy - 1},
        "right": {"gy": gy + 1},
    }
    mates = [{"ev": lax.rem(ev + d, n_ev)} for d in range(1, n_ev)]

    for side in has:

        @pl.when(has[side])
        def _(side=side):
            pl.semaphore_signal(barrier, inc=1, device_id=where[side], device_id_type=MESH)

    for mate in mates:
        pl.semaphore_signal(barrier, inc=1, device_id=mate, device_id_type=MESH)

    loads = {}

    def load(name, src, dst):
        copy = pltpu.make_async_copy(src, dst, load_sem.at[len(loads)])
        loads[name] = copy
        copy.start()

    for s, state in enumerate((fwd, adj)):
        load(("n0", s), state.at[0, pl.ds(3, 1)], ext.at[s, pl.ds(0, 1), :, pl.ds(PAD, rows), :])
        load(("n1", s), state.at[0, pl.ds(6, 2)], ext.at[s, pl.ds(1, 2), :, pl.ds(PAD, rows), :])
        load(("s0", s), state.at[0, pl.ds(4, 2)], rest.at[s, pl.ds(3, 2)])
        load(("s1", s), state.at[0, pl.ds(8, 1)], rest.at[s, pl.ds(5, 1)])
    for s, state in enumerate((fwd, adj)):
        load(("v", s), state.at[0, pl.ds(0, 3)], rest.at[s, pl.ds(0, 3)])
    load("table", table_in, table)
    load("elem", elem_in, elem)
    load("mask", mask_in, mask)
    load("buoy", buoy_in, buoy)
    load("lame", lame_in, lame)
    load("shear", shear_in, shear)

    for start in (0, PAD + rows):
        vint[:, :, :, pl.ds(start, PAD), :] = jnp.zeros(vint.shape[:3] + (PAD, cols), jnp.float32)

    @pl.when(gx == 0)
    def _():
        for ref in (ext, vext):
            ref[:, :, :, pl.ds(0, PAD), :] = jnp.zeros(ref.shape[:3] + (PAD, cols), jnp.float32)

    @pl.when(gx == n_gx - 1)
    def _():
        for ref in (ext, vext):
            ref[:, :, :, pl.ds(PAD + rows, PAD), :] = jnp.zeros(
                ref.shape[:3] + (PAD, cols), jnp.float32
            )

    @pl.when(gy == 0)
    def _():
        from_left[...] = jnp.zeros(from_left.shape, jnp.float32)

    @pl.when(gy == n_gy - 1)
    def _():
        from_right[...] = jnp.zeros(from_right.shape, jnp.float32)

    for s in range(2):
        for name in ("n0", "n1", "s0", "s1"):
            loads[name, s].wait()

    lanes = lax.broadcasted_iota(jnp.int32, (rows, cols), 1)
    edge = jnp.logical_or(lanes < 2, lanes >= cols - 2)

    def inside(ref, c):
        return ref[:, c, :, pl.ds(PAD, rows), :]

    def row_copy(ref, phase, side):
        start, goal = (PAD + rows - 2, PAD - 2) if side == "down" else (PAD, PAD + rows)
        i = 2 * phase + (side == "down")
        return pltpu.make_async_remote_copy(
            src_ref=ref.at[:, :, :, pl.ds(start, 2), :],
            dst_ref=ref.at[:, :, :, pl.ds(goal, 2), :],
            send_sem=row_send.at[i],
            recv_sem=row_recv.at[i],
            device_id=where[side],
            device_id_type=MESH,
        )

    def lane_copy(phase, side):
        i = 2 * phase + (side == "right")
        return pltpu.make_async_remote_copy(
            src_ref=pack.at[phase],
            dst_ref=(from_left if side == "right" else from_right).at[phase],
            send_sem=lane_send.at[i],
            recv_sem=lane_recv.at[i],
            device_id=where[side],
            device_id_type=MESH,
        )

    opposite = {"up": "down", "down": "up", "left": "right", "right": "left"}

    def copy_of(phase, side):
        if side in ("up", "down"):
            return row_copy((ext, vext)[phase], phase, side)
        return lane_copy(phase, side)

    def send(phase, sides):
        for side in sides:

            @pl.when(has[side])
            def _(side=side):
                copy_of(phase, side).start()

    def receive(phase, sides):
        for side in sides:

            @pl.when(has[side])
            def _(side=side):
                copy_of(phase, opposite[side]).wait_recv()

    def sent(phase):
        for side in has:

            @pl.when(has[side])
            def _(side=side):
                copy_of(phase, side).wait_send()

    sxy, syy, syz = inside(ext, 1), rest[:, 3], rest[:, 5]
    pack[0] = pack_lanes((sxy, syy, syz), lanes)

    peers = len(mates) + sum(flag.astype(jnp.int32) for flag in has.values())
    pl.semaphore_wait(barrier, peers)

    send(0, ("up", "down", "left", "right"))

    sums[0] = lane_ahead(sxy) + depth_ahead(inside(ext, 2))
    sums[1] = lane_behind(syy) + depth_ahead(syz)
    sums[2] = lane_ahead(syz) + depth_behind(rest[:, 4])

    for name in (("v", 0), ("v", 1), "table", "elem", "mask", "buoy"):
        loads[name].wait()
    entries = table.shape[2]
    chunks = [(a, min(a + cols, entries)) for a in range(0, entries, cols)]
    for z in range(depth):
        index = elem[z]
        gate = STEP * mask[z].astype(jnp.float32)
        low, high = index % cols, index // cols
        for i in range(3):
            value = jnp.zeros((rows, cols), jnp.float32)
            for j, (a, b) in enumerate(chunks):
                line = jnp.broadcast_to(table[i, :, pl.ds(a, b - a)], (rows, cols))
                value = jnp.where(high == j, jnp.take_along_axis(line, low, axis=1), value)
            rest[0, i, z] = rest[0, i, z] + gate * value

    receive(0, ("up", "down", "left", "right"))
    fix = lane_fix(pack[0], from_left[0], from_right[0], lanes, per, (True, False, True))
    force = buoy[...] * STEP
    force = jnp.stack([force, -force])
    row_diff = (row_behind, row_ahead, row_ahead)
    for i in range(3):
        divergence = (
            sums[i]
            + row_diff[i](ext, i, rows)
            + unpack_lanes(fix, i * per, per, depth, edge)
        )
        moved = rest[:, i] + force * divergence
        vext[:, i, :, pl.ds(PAD, rows), :] = moved
        new[0, i] = moved[0]

    velocity = [inside(vext, i) for i in range(3)]
    pack[1] = pack_lanes(velocity, lanes)
    send(1, ("up", "down", "left", "right"))

    def mate_copy(d, part):
        top, bottom = pl.ds(0, 2), pl.ds(rows - 2, 2)
        both = pl.ds(0, 2)
        src, dst = (
            (mine.at[2], theirs.at[d, 2]),
            (early, theirs.at[d, both]),
            (mine.at[both, :, top, :], theirs_rows.at[d, :, :, top, :]),
            (mine.at[both, :, bottom, :], theirs_rows.at[d, :, :, bottom, :]),
            (mine_lanes, theirs_lanes.at[d]),
        )[part]
        return pltpu.make_async_remote_copy(
            src_ref=src,
            dst_ref=dst,
            send_sem=ev_send.at[d, part],
            recv_sem=ev_recv.at[d, part],
            device_id=mates[d],
            device_id_type=MESH,
        )

    def to_mates(*parts):
        for d in range(len(mates)):
            for part in parts:
                mate_copy(d, part).start()

    def terms(rate_x, rate_y, rate_z, shear_xy, shear_xz, shear_yz):
        dilatation = rate_x + rate_y + rate_z
        modulus = (
            2.0 * (rate_x[0] * rate_x[1] + rate_y[0] * rate_y[1] + rate_z[0] * rate_z[1])
            + shear_xy[0] * shear_xy[1]
            + shear_xz[0] * shear_xz[1]
            + shear_yz[0] * shear_yz[1]
        )
        return dilatation, dilatation[0] * dilatation[1], modulus

    vx, vy, vz = velocity
    mine[2] = (
        vx[0] * (vx[1] - rest[1, 0]) + vy[0] * (vy[1] - rest[1, 1]) + vz[0] * (vz[1] - rest[1, 2])
    ) / STEP
    to_mates(0)

    sums[0] = lane_behind(vx)
    sums[1] = lane_ahead(vy)
    sums[2] = lane_behind(vz) + depth_behind(vy)
    rate_z = depth_ahead(vz)
    shear_xz = depth_behind(vx)

    for i in range(3):
        vint[:, i, :, pl.ds(PAD, rows), :] = velocity[i]
    _, early[0], early[1] = terms(
        row_ahead(vint, 0, rows),
        sums[1],
        rate_z,
        sums[0] + row_behind(vint, 1, rows),
        shear_xz + row_behind(vint, 2, rows),
        sums[2],
    )
    to_mates(1)
    loads["lame"].wait()
    loads["shear"].wait()

    receive(1, ("up", "down", "left", "right"))
    fix = lane_fix(pack[1], from_left[1], from_right[1], lanes, per, (False, True, False))
    rate_x = row_ahead(vext, 0, rows)
    rate_y = sums[1] + unpack_lanes(fix, per, per, depth, edge)
    shear_xy = sums[0] + unpack_lanes(fix, 0, per, depth, edge) + row_behind(vext, 1, rows)
    shear_xz = shear_xz + row_behind(vext, 2, rows)
    shear_yz = sums[2] + unpack_lanes(fix, 2 * per, per, depth, edge)
    dilatation, mine[0], mine[1] = terms(rate_x, rate_y, rate_z, shear_xy, shear_xz, shear_yz)
    to_mates(2, 3)
    mine_lanes[...] = pack_lanes((mine[pl.ds(0, 2)],), lanes)
    to_mates(4)

    mu = STEP * shear[...]
    bulk = STEP * lame[...] * dilatation[0]
    new[0, 3] = ext[0, 0, :, pl.ds(PAD, rows), :] + (bulk + 2.0 * mu * rate_x[0])
    new[0, 4] = rest[0, 3] + (bulk + 2.0 * mu * rate_y[0])
    new[0, 5] = rest[0, 4] + (bulk + 2.0 * mu * rate_z[0])
    new[0, 6] = ext[0, 1, :, pl.ds(PAD, rows), :] + mu * shear_xy[0]
    new[0, 7] = ext[0, 2, :, pl.ds(PAD, rows), :] + mu * shear_xz[0]
    new[0, 8] = rest[0, 5] + mu * shear_yz[0]
    for d in range(len(mates)):
        for part in range(5):
            mate_copy(d, part).wait_recv()
    sent(0)
    sent(1)
    for d in range(len(mates)):
        for part in range(5):
            mate_copy(d, part).wait_send()


def finish(n_mates, new_in, mine, theirs, theirs_rows, theirs_lanes, out, grad, total, sem):
    state_copy = pltpu.make_async_copy(new_in, out, sem.at[0])
    state_copy.start()
    _, depth, rows, cols = mine.shape
    lanes = lax.broadcasted_iota(jnp.int32, (rows, cols), 1)
    edge = jnp.logical_or(lanes < 2, lanes >= cols - 2)
    for part in range(3):
        for z in range(depth):
            value = mine[part, z]
            for d in range(n_mates):
                other = theirs[d, part, z]
                if part < 2:
                    last = turn(theirs_lanes[d], -(4 * (part * depth + z) + 2))
                    other = jnp.where(edge, last, other)
                value = value + other
            total[part, z] = value
    if n_mates:
        for start in (0, rows - 2):
            ends = pl.ds(start, 2)
            value = mine[pl.ds(0, 2), :, ends, :]
            for d in range(n_mates):
                value = value + theirs_rows[d, :, :, ends, :]
            total[pl.ds(0, 2), :, ends, :] = value
    grad_copy = pltpu.make_async_copy(total, grad, sem.at[1])
    grad_copy.start()
    state_copy.wait()
    grad_copy.wait()


def solution(mesh):
    sizes = (mesh.shape["ev"], mesh.shape["gx"], mesh.shape["gy"])

    def shards(fwd, adj, lame, shear, buoy, mask, elem, table):
        _, _, depth, rows, cols = fwd.shape
        table = jnp.swapaxes(table, 0, 1)
        block = (depth, rows, cols)
        padded = (2, 3, depth, rows + 2 * PAD, cols)
        mates = max(sizes[0] - 1, 1)
        f32 = jnp.float32
        dma = pltpu.SemaphoreType.DMA
        anywhere = pl.BlockSpec(memory_space=pl.ANY)
        whole = pl.BlockSpec(memory_space=pltpu.VMEM)
        new, *pieces = pl.pallas_call(
            functools.partial(kernel, sizes),
            out_shape=(
                pltpu.VMEM(fwd.shape, f32),
                pltpu.VMEM((3,) + block, f32),
                pltpu.VMEM((mates, 3) + block, f32),
                pltpu.VMEM((mates, 2) + block, f32),
                pltpu.VMEM((mates, rows, cols), f32),
            ),
            in_specs=[anywhere] * 8,
            out_specs=(whole,) * 5,
            scratch_shapes=[
                pltpu.VMEM(padded, f32),
                pltpu.VMEM((2, 6) + block, f32),
                pltpu.VMEM(block, f32),
                pltpu.VMEM(block, f32),
                pltpu.VMEM(block, f32),
                pltpu.VMEM(block, jnp.int32),
                pltpu.VMEM(block, jnp.int32),
                pltpu.VMEM(table.shape, f32),
                pltpu.VMEM(padded, f32),
                pltpu.VMEM((3, 2) + block, f32),
                pltpu.VMEM((2, rows, cols), f32),
                pltpu.VMEM((2, rows, cols), f32),
                pltpu.VMEM((2, rows, cols), f32),
                pltpu.VMEM(padded, f32),
                pltpu.VMEM((2,) + block, f32),
                pltpu.VMEM((rows, cols), f32),
                dma((16,)),
                dma((4,)),
                dma((4,)),
                dma((4,)),
                dma((4,)),
                dma((mates, 5)),
                dma((mates, 5)),
            ],
            compiler_params=pltpu.CompilerParams(
                collective_id=0, has_side_effects=True, vmem_limit_bytes=56 * 1024 * 1024
            ),
        )(fwd, adj, lame, shear, buoy, mask, elem, table)
        return pl.pallas_call(
            functools.partial(finish, sizes[0] - 1),
            out_shape=(
                jax.ShapeDtypeStruct(fwd.shape, f32),
                jax.ShapeDtypeStruct((3,) + block, f32),
            ),
            in_specs=[anywhere] + [whole] * 4,
            out_specs=(anywhere, anywhere),
            scratch_shapes=[pltpu.VMEM((3,) + block, f32), dma((2,))],
            compiler_params=pltpu.CompilerParams(vmem_limit_bytes=8 * 1024 * 1024),
        )(new, *pieces)

    grid = P(None, "gx", "gy")
    state = P("ev", None, None, "gx", "gy")
    return jax.shard_map(
        shards,
        mesh=mesh,
        in_specs=(state, state, grid, grid, grid, grid, grid, P("ev", None, None)),
        out_specs=(state, P(None, None, "gx", "gy")),
        check_vma=False,
    )
```

profile of v0, /device:TPU:0, one launch (start us, length us, event | category | flops | bytes accessed | tf_op | source)
XLA Modules:
  0.0 15.4 jit_solution(14724159438518109854)
XLA Ops:
  0.6 14.0 %shard_map.95 = (f32[1,9,4,16,128]{4,3,2,1,0:T(8,128)S(1)}, f32[3,4,16,128]{3,2,1,0:T(8,128)S(1)}, f32[1,3,4,16,128]{4,3,2,1,0:T(8,128)S(1)}, f32[1,2,4,16,128]{4,3,2,1,0:T(8,128)S(1)}, f32[1,16,128]{2,1,0:T(8,128)S(1)}) custom-call(f32[1,9,4,16,128]{4,3,2,1,0:T(8,128)} %fwd.1, f32[1,9,4,16,128]{4,3,2,1,0:T(8,128)} %adj.1, f32[4,16,128]{2,1,0:T(8,128)} %lame_in.1, ...), custom_call_target="tpu_custom_call" | custom-call | tf_op jit(solution)/shard_map/pallas_call | solution.py:461
  14.6 0.8 %shard_map.96 = (f32[1,9,4,16,128]{4,3,2,1,0:T(8,128)}, f32[3,4,16,128]{3,2,1,0:T(8,128)}) custom-call(f32[1,9,4,16,128]{4,3,2,1,0:T(8,128)S(1)} %get-tuple-element.7.new_in, f32[3,4,16,128]{3,2,1,0:T(8,128)S(1)} %get-tuple-element.8.mine, f32[1,3,4,16,128]{4,3,2,1,0:T(8,128)S(1)} %get-tuple-element.9.theirs, ...), custom_call_target="tpu_custom_call" | custom-call | tf_op jit(solution)/shard_map/pallas_call | solution.py:501
where the time goes:
time: 15.6 us; the launch traced here: 15.4 us
  Pallas kernels  14.8 us (95%)
  between operations  0.64 us (4%)
    pallas_call x1, Pallas kernels, shards(): pl.pallas_call(functools.partial(kernel, sizes), out_shape=(pltpu.VMEM(fw...  14 us
    pallas_call x1, Pallas kernels, shards(): pl.pallas_call(functools.partial(finish, sizes[0] - 1), out_shape=(jax.Sh...  0.76 us

commit v1 on v0

--- a/solution.py
+++ b/solution.py
@@ -187,18 +187,6 @@
         load(("n1", s), state.at[0, pl.ds(6, 2)], ext.at[s, pl.ds(1, 2), :, pl.ds(PAD, rows), :])
         load(("s0", s), state.at[0, pl.ds(4, 2)], rest.at[s, pl.ds(3, 2)])
         load(("s1", s), state.at[0, pl.ds(8, 1)], rest.at[s, pl.ds(5, 1)])
-    for s, state in enumerate((fwd, adj)):
-        load(("v", s), state.at[0, pl.ds(0, 3)], rest.at[s, pl.ds(0, 3)])
-    load("table", table_in, table)
-    load("elem", elem_in, elem)
-    load("mask", mask_in, mask)
-    load("buoy", buoy_in, buoy)
-    load("lame", lame_in, lame)
-    load("shear", shear_in, shear)
-
-    for start in (0, PAD + rows):
-        vint[:, :, :, pl.ds(start, PAD), :] = jnp.zeros(vint.shape[:3] + (PAD, cols), jnp.float32)
-
     @pl.when(gx == 0)
     def _():
         for ref in (ext, vext):
@@ -287,6 +275,18 @@
     pl.semaphore_wait(barrier, peers)
 
     send(0, ("up", "down", "left", "right"))
+
+    for s, state in enumerate((fwd, adj)):
+        load(("v", s), state.at[0, pl.ds(0, 3)], rest.at[s, pl.ds(0, 3)])
+    load("table", table_in, table)
+    load("elem", elem_in, elem)
+    load("mask", mask_in, mask)
+    load("buoy", buoy_in, buoy)
+    load("lame", lame_in, lame)
+    load("shear", shear_in, shear)
+
+    for start in (0, PAD + rows):
+        vint[:, :, :, pl.ds(start, PAD), :] = jnp.zeros(vint.shape[:3] + (PAD, cols), jnp.float32)
 
     sums[0] = lane_ahead(sxy) + depth_ahead(inside(ext, 2))
     sums[1] = lane_behind(syy) + depth_ahead(syz)

time: 15.6 us -> 15.6 us (level)
  no operation moved by 1% of the time
where the time goes in v1:
time: 15.6 us; the launch traced here: 15.4 us
  Pallas kernels  14.8 us (95%)
  between operations  0.64 us (4%)
    pallas_call x1, Pallas kernels, shards(): pl.pallas_call(functools.partial(kernel, sizes), out_shape=(pltpu.VMEM(fw...  14 us
    pallas_call x1, Pallas kernels, shards(): pl.pallas_call(functools.partial(finish, sizes[0] - 1), out_shape=(jax.Sh...  0.76 us

profile of v1, /device:TPU:0, one launch (start us, length us, event | category | flops | bytes accessed | tf_op | source)
XLA Modules:
  0.0 15.4 jit_solution(11910107775579316522)
XLA Ops:
  0.6 14.0 %shard_map.95 = (f32[1,9,4,16,128]{4,3,2,1,0:T(8,128)S(1)}, f32[3,4,16,128]{3,2,1,0:T(8,128)S(1)}, f32[1,3,4,16,128]{4,3,2,1,0:T(8,128)S(1)}, f32[1,2,4,16,128]{4,3,2,1,0:T(8,128)S(1)}, f32[1,16,128]{2,1,0:T(8,128)S(1)}) custom-call(f32[1,9,4,16,128]{4,3,2,1,0:T(8,128)} %fwd.1, f32[1,9,4,16,128]{4,3,2,1,0:T(8,128)} %adj.1, f32[4,16,128]{2,1,0:T(8,128)} %lame_in.1, ...), custom_call_target="tpu_custom_call" | custom-call | tf_op jit(solution)/shard_map/pallas_call | solution.py:461
  14.6 0.8 %shard_map.96 = (f32[1,9,4,16,128]{4,3,2,1,0:T(8,128)}, f32[3,4,16,128]{3,2,1,0:T(8,128)}) custom-call(f32[1,9,4,16,128]{4,3,2,1,0:T(8,128)S(1)} %get-tuple-element.7.new_in, f32[3,4,16,128]{3,2,1,0:T(8,128)S(1)} %get-tuple-element.8.mine, f32[1,3,4,16,128]{4,3,2,1,0:T(8,128)S(1)} %get-tuple-element.9.theirs, ...), custom_call_target="tpu_custom_call" | custom-call | tf_op jit(solution)/shard_map/pallas_call | solution.py:501
